TPU v7x, 32 devices: a whole 2x2x4 slice. The times are simulated.
32 devices in a mesh: dp: 16 (over z, x, core), tensor: 2 (over y).
Axes of the slice: x: 2, y: 2, z: 4, core: 2. Of those that a mesh axis runs over, the one named last changes fastest.
Arguments:
- hidden: bfloat16 [32, 1024, 1024], P('dp'), may hold values from -6 to 6
- segment_ids: int32 [32, 1024], P('dp'), may hold values from 0 to 3, never falling along the last dimension, each value on 1 to 800 neighbouring positions
- norm_gain: float32 [1024], replicated, may hold values from 0.1 to 1.9
- proj_gate: bfloat16 [1024, 2048], P(None, 'tensor'), may hold values from -0.1875 to 0.1875
- proj_value: bfloat16 [1024, 2048], P(None, 'tensor'), may hold values from -0.1875 to 0.1875
- proj_state: bfloat16 [1024, 256], replicated, may hold values from -0.1875 to 0.1875
- proj_step: bfloat16 [1024, 32], P(None, 'tensor'), may hold values from -0.1875 to 0.1875
- conv_value: float32 [4, 2048], P(None, 'tensor'), may hold values from -3 to 3
- conv_value_bias: float32 [2048], P('tensor'), may hold values from -3 to 3
- conv_state: float32 [4, 256], replicated, may hold values from -3 to 3
- conv_state_bias: float32 [256], replicated, may hold values from -3 to 3
- step_bias: float32 [32], P('tensor'), may hold values from -6 to -2
- decay_log: float32 [32], P('tensor'), may hold values from 0 to 2.77
- skip_gain: float32 [32], P('tensor'), may hold values from 0.5 to 1.5
- gate_gain: float32 [2048], P('tensor'), may hold values from 0.1 to 1.9
- proj_out: bfloat16 [1024, 2048], P(None, 'tensor'), may hold values from -0.125 to 0.125
- out_grad: bfloat16 [32, 1024, 1024], P('dp'), may hold values from -6 to 6
Outputs:
- block_out: bfloat16 [32, 1024, 1024], P('dp')
- grad_hidden: float32 [32, 1024, 1024], P('dp')
- grad_norm_gain: float32 [1024], replicated
- grad_proj_gate: float32 [1024, 2048], P('dp', 'tensor')
- grad_proj_value: float32 [1024, 2048], P('dp', 'tensor')
- grad_proj_state: float32 [1024, 256], P('dp')
- grad_proj_step: float32 [1024, 32], P('dp', 'tensor')
- grad_conv_value: float32 [4, 2048], P(None, 'tensor')
- grad_conv_value_bias: float32 [2048], P('tensor')
- grad_conv_state: float32 [4, 256], replicated
- grad_conv_state_bias: float32 [256], replicated
- grad_step_bias: float32 [32], P('tensor')
- grad_decay_log: float32 [32], P('tensor')
- grad_skip_gain: float32 [32], P('tensor')
- grad_gate_gain: float32 [2048], P('tensor')
- grad_proj_out: float32 [1024, 2048], P('dp', 'tensor')
Inputs may be any that keep to these rules, and one draw needn't show every extreme that they name: `segment_ids`: tokens of a sequence with the same number form one document; numbers never fall along a sequence; each sequence holds 4 documents of 1 to 800 tokens, one of exactly 800.
All inputs are finite; a program needn't handle non-finite values.
Results may differ from a plain program's by a relative error of at most 0.019.
Values sent between devices are 32-bit elements; how exact they have to be, the bound alone decides.
A program may use at most 192 MiB of HBM per device.

v0:
```python
import functools
import jax
import jax.numpy as jnp
from jax import lax
from jax.sharding import PartitionSpec as P

HEAD_DIM = 64
STATE = 128
KERNEL = 4
epsilon = 1e-05
precise = lax.Precision.HIGHEST


def lag_masks(segment_row):
    length = segment_row.shape[0]
    result = [jnp.ones((length,), jnp.float32)]
    for delay in range(1, KERNEL):
        earlier = jnp.concatenate(
            [jnp.full((delay,), -1, jnp.int32), segment_row[: length - delay]]
        )
        result.append((earlier == segment_row).astype(jnp.float32))
    return result


def causal_conv(values, weight, conv_bias, doc_masks):
    length = values.shape[0]
    summed = conv_bias[None, :] + weight[KERNEL - 1][None, :] * values
    for delay in range(1, KERNEL):
        earlier = jnp.concatenate(
            [jnp.zeros((delay, values.shape[1]), jnp.float32), values[: length - delay]], axis=0
        )
        summed = summed + weight[KERNEL - 1 - delay][None, :] * earlier * doc_masks[delay][:, None]
    return jax.nn.silu(summed)


CHUNK = 128


def head_mix(values, states, step_raw, segment_row, step_bias, decay_log, skip_gain):
    length, inner = values.shape
    heads = step_raw.shape[1]
    chunks = length // CHUNK
    step_size = jax.nn.softplus(step_raw + step_bias[None, :])
    decay_rate = -jnp.exp(decay_log)
    places = jnp.arange(CHUNK)
    lower = places[:, None] >= places[None, :]
    drop = (step_size * decay_rate[None, :]).reshape(chunks, CHUNK, heads)
    running = jnp.einsum("ts,csh->cth", lower.astype(jnp.float32), drop, precision=precise)
    segments = segment_row.reshape(chunks, CHUNK)
    last = segments[:, -1]
    before = jnp.concatenate([jnp.full((1,), -1, jnp.int32), last[:-1]])
    allowed = lower[None] & (segments[:, :, None] == segments[:, None, :])
    state_in = states[:, :STATE].astype(jnp.bfloat16).reshape(chunks, CHUNK, STATE)
    state_out = states[:, STATE:].astype(jnp.bfloat16).reshape(chunks, CHUNK, STATE)
    affinity = jnp.einsum("ctn,csn->cts", state_out, state_in, preferred_element_type=jnp.float32)
    running_head = running.transpose(0, 2, 1)
    step_head = step_size.reshape(chunks, CHUNK, heads).transpose(0, 2, 1)
    decays = jnp.exp(
        jnp.where(
            allowed[:, None], running_head[:, :, :, None] - running_head[:, :, None, :], -1e30
        )
    )
    mixing = (decays * affinity[:, None] * step_head[:, :, None, :]).astype(jnp.bfloat16)
    low_head = values.astype(jnp.bfloat16).reshape(chunks, CHUNK, heads, HEAD_DIM)
    near = jnp.einsum("chts,cshp->cthp", mixing, low_head, preferred_element_type=jnp.float32)
    near = near.reshape(chunks, CHUNK, inner)
    spread = (jnp.arange(inner)[None, :] // HEAD_DIM == jnp.arange(heads)[:, None]).astype(
        jnp.float32
    )
    total = running[:, -1, :]
    at_end = (segments == last[:, None]).astype(jnp.float32)
    from_start = (segments == before[:, None]).astype(jnp.float32)
    keep_scale = (
        jnp.exp(total[:, None, :] - running)
        * step_size.reshape(chunks, CHUNK, heads)
        * at_end[:, :, None]
    )
    read_scale = jnp.exp(running) * from_start[:, :, None]
    carry = jnp.exp(total) * (last == before).astype(jnp.float32)[:, None]
    keep_wide = jnp.einsum("cth,hi->cti", keep_scale, spread, precision=lax.Precision.HIGH)
    read_wide = jnp.einsum("cth,hi->cti", read_scale, spread, precision=lax.Precision.HIGH)
    carry_wide = jnp.einsum("ch,hi->ci", carry, spread, precision=precise)
    kept = (values.reshape(chunks, CHUNK, inner) * keep_wide).astype(jnp.bfloat16)
    gained = jnp.einsum("csn,csi->cni", state_in, kept, preferred_element_type=jnp.float32)
    held = jnp.zeros((STATE, inner), jnp.float32)
    entry = []
    for c in range(chunks):
        entry.append(held.astype(jnp.bfloat16))
        held = held * carry_wide[c][None, :] + gained[c]
    entry = jnp.stack(entry)
    far = jnp.einsum("ctn,cni->cti", state_out, entry, preferred_element_type=jnp.float32)
    mixed = (near + far * read_wide).reshape(length, inner)
    return mixed + jnp.repeat(skip_gain, HEAD_DIM)[None, :] * values


def mixer(
    segment_row,
    value_row,
    state_row,
    step_row,
    conv_value,
    conv_value_bias,
    conv_state,
    conv_state_bias,
    step_bias,
    decay_log,
    skip_gain,
):
    doc_masks = lag_masks(segment_row)
    value_conv = causal_conv(value_row, conv_value, conv_value_bias, doc_masks)
    state_conv = causal_conv(state_row, conv_state, conv_state_bias, doc_masks)
    return head_mix(value_conv, state_conv, step_row, segment_row, step_bias, decay_log, skip_gain)


def right_product(left, weight):
    return lax.dot_general(
        left, weight, (((1,), (1,)), ((), ())), preferred_element_type=jnp.float32
    )


def token_product(left, right):
    return lax.dot_general(
        left, right, (((0,), (0,)), ((), ())), preferred_element_type=jnp.float32
    )


def tensor_sum(part):
    count = lax.axis_size("tensor")
    if count == 1:
        return part
    if count == 2:
        return part + lax.ppermute(part, "tensor", [(0, 1), (1, 0)])
    return lax.psum(part, "tensor")


def local(
    hidden,
    segment_ids,
    norm_gain,
    proj_gate,
    proj_value,
    proj_state,
    proj_step,
    conv_value,
    conv_value_bias,
    conv_state,
    conv_state_bias,
    step_bias,
    decay_log,
    skip_gain,
    gate_gain,
    proj_out,
    out_grad,
):
    seq_count, length, width = hidden.shape
    local_inner = proj_gate.shape[1]
    local_heads = proj_step.shape[1]
    state_width = proj_state.shape[1]
    tensor_count = lax.axis_size("tensor")
    inner_total = local_inner * tensor_count
    every = range(seq_count)
    wides = [hidden[s].astype(jnp.float32) for s in every]
    row_scales = [lax.rsqrt(jnp.mean(w * w, axis=-1, keepdims=True) + epsilon) for w in wides]
    normeds = [(w * r * norm_gain[None, :]).astype(jnp.bfloat16) for w, r in zip(wides, row_scales)]
    params = (
        conv_value,
        conv_value_bias,
        conv_state,
        conv_state_bias,
        step_bias,
        decay_log,
        skip_gain,
    )
    gate_raws, mixed_outs, mixer_backs, gateds, squares = ([], [], [], [], [])
    for s in every:
        gate_raw = jnp.dot(normeds[s], proj_gate, preferred_element_type=jnp.float32)
        value_raw = jnp.dot(normeds[s], proj_value, preferred_element_type=jnp.float32)
        state_raw = jnp.dot(normeds[s], proj_state, preferred_element_type=jnp.float32)
        step_raw = jnp.dot(normeds[s], proj_step, preferred_element_type=jnp.float32)
        mixed_out, back = jax.vjp(
            jax.checkpoint(functools.partial(mixer, segment_ids[s])),
            value_raw,
            state_raw,
            step_raw,
            *params
        )
        gated = mixed_out * jax.nn.silu(gate_raw)
        gate_raws.append(gate_raw)
        mixed_outs.append(mixed_out)
        mixer_backs.append(back)
        gateds.append(gated)
        squares.append(jnp.sum(gated * gated, axis=-1))
    d_output_ins = [
        jnp.dot(out_grad[s], proj_out, preferred_element_type=jnp.float32) for s in every
    ]
    inners = [jnp.sum(d_output_ins[s] * gate_gain[None, :] * gateds[s], axis=-1) for s in every]
    both = lax.psum(jnp.stack(squares + inners), "tensor")
    block_outs, output_ins, d_gates, d_mixeds = ([], [], [], [])
    grad_gate_gain = jnp.zeros((local_inner,), jnp.float32)
    for s in every:
        gated, gate_raw = (gateds[s], gate_raws[s])
        gated_scale = lax.rsqrt(both[s] / inner_total + epsilon)[:, None]
        gate_inner = both[seq_count + s][:, None]
        output_in = (gated * gated_scale * gate_gain[None, :]).astype(jnp.bfloat16)
        branch = tensor_sum(right_product(output_in, proj_out))
        block_outs.append((wides[s] + branch).astype(jnp.bfloat16))
        d_output_in = d_output_ins[s]
        grad_gate_gain = grad_gate_gain + jnp.sum(d_output_in * gated * gated_scale, axis=0)
        weighted = d_output_in * gate_gain[None, :]
        d_gated = gated_scale * weighted - gated_scale**3 * gated * gate_inner / inner_total
        sigma = jax.nn.sigmoid(gate_raw)
        d_mixeds.append(d_gated * gate_raw * sigma)
        d_gates.append(
            (d_gated * mixed_outs[s] * sigma * (1.0 + gate_raw * (1.0 - sigma))).astype(
                jnp.bfloat16
            )
        )
        output_ins.append(output_in)
    normed_all = jnp.concatenate(normeds, axis=0)
    early = lax.psum_scatter(
        jnp.concatenate(
            [
                token_product(normed_all, jnp.concatenate(d_gates, axis=0)),
                token_product(
                    out_grad.reshape(seq_count * length, width), jnp.concatenate(output_ins, axis=0)
                ),
            ],
            axis=1,
        ),
        "dp",
        scatter_dimension=0,
        tiled=True,
    )
    late_weight = jnp.concatenate([proj_value, proj_state, proj_step], axis=1)
    param_grads, lates, grad_hiddens = (None, [], [])
    grad_norm_gain = jnp.zeros((width,), jnp.float32)
    for s in every:
        d_value, d_state, d_step, *grads = mixer_backs[s](d_mixeds[s])
        param_grads = grads if s == 0 else [a + b for a, b in zip(param_grads, grads)]
        late = jnp.concatenate([d_value, d_state, d_step], axis=1).astype(jnp.bfloat16)
        lates.append(late)
        part = right_product(d_gates[s], proj_gate) + right_product(late, late_weight)
        row_scale, wide = (row_scales[s], wides[s])
        grad_norm_gain = grad_norm_gain + jnp.sum(part * wide * row_scale, axis=0)
        d_scaled = tensor_sum(part) * norm_gain[None, :]
        norm_inner = jnp.sum(d_scaled * wide, axis=-1, keepdims=True)
        grad_hiddens.append(
            out_grad[s].astype(jnp.float32)
            + row_scale * d_scaled
            - row_scale**3 * wide * norm_inner / width
        )
    later = lax.psum_scatter(
        token_product(normed_all, jnp.concatenate(lates, axis=0)),
        "dp",
        scatter_dimension=0,
        tiled=True,
    )
    edge_state = local_inner + state_width
    grad_proj_state = lax.psum(later[:, local_inner:edge_state], "tensor")
    g_cv, g_cvb, g_cs, g_csb, g_sb, g_dl, g_sg = param_grads
    own = [g_cv, g_cvb, g_sb, g_dl, g_sg, grad_gate_gain]
    shared = [g_cs, g_csb, grad_norm_gain]
    own_flat = jnp.concatenate([g.reshape(-1) for g in own])
    place = lax.axis_index("tensor")
    mine = (jnp.arange(tensor_count) == place)[:, None]
    slots = jnp.where(mine, own_flat[None, :], 0.0).reshape(-1)
    packed = lax.psum(jnp.concatenate([slots] + [g.reshape(-1) for g in shared]), ("dp", "tensor"))
    own_sum = lax.dynamic_slice(packed, (place * own_flat.shape[0],), (own_flat.shape[0],))
    shared_sum = packed[slots.shape[0] :]

    def split(flat, like):
        result, edge = ([], 0)
        for g in like:
            result.append(flat[edge : edge + g.size].reshape(g.shape))
            edge += g.size
        return result

    r_cv, r_cvb, r_sb, r_dl, r_sg, r_gg = split(own_sum, own)
    r_cs, r_csb, r_ng = split(shared_sum, shared)
    return (
        jnp.stack(block_outs),
        jnp.stack(grad_hiddens),
        r_ng,
        early[:, :local_inner],
        later[:, :local_inner],
        grad_proj_state,
        later[:, edge_state:],
        r_cv,
        r_cvb,
        r_cs,
        r_csb,
        r_sb,
        r_dl,
        r_sg,
        r_gg,
        early[:, local_inner:],
    )


def solution(mesh):
    in_specs = (
        P("dp", None, None),
        P("dp", None),
        P(),
        P(None, "tensor"),
        P(None, "tensor"),
        P(),
        P(None, "tensor"),
        P(None, "tensor"),
        P("tensor"),
        P(),
        P(),
        P("tensor"),
        P("tensor"),
        P("tensor"),
        P("tensor"),
        P(None, "tensor"),
        P("dp", None, None),
    )
    out_specs = (
        P("dp", None, None),
        P("dp", None, None),
        P(),
        P("dp", "tensor"),
        P("dp", "tensor"),
        P("dp", None),
        P("dp", "tensor"),
        P(None, "tensor"),
        P("tensor"),
        P(),
        P(),
        P("tensor"),
        P("tensor"),
        P("tensor"),
        P("tensor"),
        P("dp", "tensor"),
    )
    return jax.shard_map(local, mesh=mesh, in_specs=in_specs, out_specs=out_specs, check_vma=False)
```

profile of v0, /device:TPU:0, one launch (start us, length us, event | category | flops | bytes accessed | tf_op | source)
XLA Modules:
  0.0 1003.6 jit_solution(18028607774672307865)
XLA Ops:
  55.0 22.0 %fusion.446 = (bf16[1024,1024]{1,0:T(8,128)(2,1)}, f32[1024,1024]{1,0:T(8,128)}, bf16[1024,1024]{1,0:T(8,128)(2,1)}, f32[1024,1024]{1,0:T(8,128)S(1)}) fusion(f32[1024]{0:T(1024)S(1)} %get-tuple-element.459, f32[1021,1024]{1,0:T(8,128)} %bitcast.712, f32[1024]{0:T(1024)} %bitcast.949, f32[1024]{0:T(1024)S(1)} %get-tuple-element.458, ...), kind=kLoop, calls=%fused_computation.727 | loop fusion | flops 33554432 | bytes 46133248 | tf_op jit(solution)/shard_map/jvp()/convert_element_type | solution.py:64
  84.3 6.5 reshape.1877
  91.8 7.6 fusion.31
  116.0 6.4 reshape.1876
  122.4 7.7 fusion.30
  150.5 15.0 %multiply_reduce_fusion.15 = (f32[1024]{0:T(1024)S(1)}, f32[1024]{0:T(1024)S(1)}, f32[1024,1024]{1,0:T(8,128)}, f32[1024]{0:T(1024)S(1)}, f32[1024]{0:T(1024)S(1...) fusion(f32[1024]{0:T(1024)S(1)} %copy-done.246, f32[1024,1024]{1,0:T(8,128)} %fusion.476, ...), kind=kOutput, calls=%fused_computation.180 | convolution fusion | flops 2172645376 | bytes 46161920 | tf_op jit(solution)/shard_map/dot_general | solution.py:194
  165.5 9.7 psum.21
  175.2 21.0 %multiply_multiply_fusion.1 = (f32[1024,1024]{1,0:T(8,128)}, bf16[1024,1024]{1,0:T(8,128)(2,1)}, f32[1024]{0:T(1024)}, bf16[1024,1024]{1,0:T(8,128)(2,1)}, bf16[...) fusion(f32[1024,1024]{1,0:T(8,128)} %fusion.476, ...), kind=kLoop, calls=%fused_computation.163 | loop fusion | flops 54523904 | bytes 58761216 | tf_op jit(solution)/shard_map/mul | solution.py:212
  220.1 13.7 %multiply_reduce_fusion.2 = (f32[1024]{0:T(1024)}, f32[1024,1024]{1,0:T(8,128)S(1)}, f32[1024,1024]{1,0:T(8,128)}) fusion(f32[1024,1024]{1,0:T(8,128)} %get-tuple-element.60, f32[1024]{0:T(1024)S(1)} %copy-done.154, f32[1021,1024]{1,0:T(8,128)} %bitcast.724, f32[1024]{0:T(1024)S(1)} %bitcast.926, f32[1024]{0:T(1024)S(1)} %copy-done.147, ...), kind=kLoop, calls=%fused_computation.124 | loop fusion | flops 17824768 | bytes 29372416 | tf_op jit(solution)/shard_map/transpose(jvp(jvp()))/checkpoint/reduce_sum | solution.py:93
  273.6 13.7 %multiply_reduce_fusion.3 = (f32[1024]{0:T(1024)}, f32[1024,1024]{1,0:T(8,128)S(1)}, f32[1024,1024]{1,0:T(8,128)}) fusion(f32[1024,1024]{1,0:T(8,128)} %get-tuple-element.46, f32[1024]{0:T(1024)S(1)} %copy-done.151, f32[1021,1024]{1,0:T(8,128)} %bitcast.715, f32[1024]{0:T(1024)S(1)} %bitcast.920, f32[1024]{0:T(1024)S(1)} %copy-done.140, ...), kind=kLoop, calls=%fused_computation.125 | loop fusion | flops 17824768 | bytes 29372416 | tf_op jit(solution)/shard_map/transpose(jvp(jvp()))/checkpoint/reduce_sum | solution.py:93
  304.9 6.0 convert_bitcast_fusion
  311.0 7.1 copy.348
  318.1 7.6 reshape.1880
  325.9 9.8 multiply_reduce_fusion.7
  349.6 6.4 reshape.1881
  356.0 11.5 %fusion.17 = (f32[8,16,128]{2,1,0:T(8,128)}, f32[8,16,128]{2,1,0:T(8,128)}, f32[8,16,128]{2,1,0:T(8,128)S(1)}, bf16[8,128,128]{2,1,0:T(8,128)(2,1)S(1)}) fusion(f32[8,16,128]{2,1,0:T(8,128)S(1)} %copy-done.170, f32[8,128,128]{2,1,0:T(8,128)} %fusion.491, f32[8,16,128]{2,1,0:T(8,128)S(1)} %fusion.299, pred[8,128,128]{2,1,0:T(8,128)(4,1)S(1)} %copy-done.117, ...), kind=kOutput, calls=%fused_computation.41 | convolution fusion | flops 297615360 | bytes 5439488 | tf_op jit(solution)/shard_map/transpose(jvp(jvp()))/checkpoint/chts,cshp->cthp/dot_general | solution.py:65
  400.7 7.1 copy.345
  407.9 7.6 reshape.1878
  415.6 10.0 %multiply_reduce_fusion.11 = (f32[1024]{0:T(1024)}, f32[1024,1024]{1,0:T(8,128)S(1)}, f32[1024,1024]{1,0:T(8,128)S(1)}) fusion(f32[1021,1024]{1,0:T(8,128)} %bitcast.718, f32[1024]{0:T(1024)S(1)} %copy-done.152, f32[1024,1024]{1,0:T(8,128)} %get-tuple-element.213, f32[1024,1024]{1,0:T(8,128)} %reshape.1878, f32[8,128,1024]{2,1,0:T(8,128)} %get-tuple-element.302, ...), kind=kLoop, calls=%fused_computation.133 | loop fusion | flops 15727616 | bytes 29360128 | tf_op jit(solution)/shard_map/transpose(jvp(jvp()))/checkpoint/reduce_sum | solution.py:32
  439.6 6.4 reshape.1879
  446.0 11.4 %fusion.15 = (f32[8,16,128]{2,1,0:T(8,128)}, f32[8,16,128]{2,1,0:T(8,128)}, f32[8,16,128]{2,1,0:T(8,128)S(1)}, bf16[8,128,128]{2,1,0:T(8,128)(2,1)S(1)}) fusion(f32[8,16,128]{2,1,0:T(8,128)S(1)} %copy-done.168, f32[8,128,128]{2,1,0:T(8,128)S(1)} %copy-done.96, f32[8,16,128]{2,1,0:T(8,128)S(1)} %fusion.302, pred[8,128,128]{2,1,0:T(8,128)(4,1)S(1)} %copy-done.115, ...), kind=kOutput, calls=%fused_computation.39 | convolution fusion | flops 297615360 | bytes 5439488 | tf_op jit(solution)/shard_map/transpose(jvp(jvp()))/checkpoint/chts,cshp->cthp/dot_general | solution.py:65
  483.7 8.6 fusion.432
  506.0 11.0 %fusion.18 = f32[1024,1296]{1,0:T(8,128)} fusion(bf16[1024,16]{1,0:T(8,128)(2,1)S(1)} %copy-done.104, bf16[1024,256]{1,0:T(8,128)(2,1)S(1)} %copy-done.90, bf16[1024,1024]{1,0:T(8,128)(2,1)S(1)} %get-tuple-element.293, bf16[1024,16]{1,0:T(8,128)(2,1)S(1)} %get-tuple-element.217, bf16[1024,256]{1,0:T(8,128)(2,1)S(1)} %get-tuple-element.306, ...), kind=kOutput, calls=%fused_computation.44 | convolution fusion | flops 5476057088 | bytes 14811136 | tf_op jit(solution)/shard_map/dot_general | solution.py:122
  517.5 8.2 fusion.62
  534.6 9.4 copy.351
  577.4 71.6 %collective-permute-done.3 = f32[1024,1024]{1,0:T(8,128)} collective-permute-done((f32[1024,1024]{1,0:T(8,128)}, f32[1024,1024]{1,0:T(8,128)}, u32[]{:S(2)}, u32[]{:S(2)}) %collective-permute-start.3) | collective-permute-done | bytes 4194336 | tf_op jit(solution)/shard_map/ppermute | solution.py:132
  649.0 89.9 %collective-permute-done.2 = f32[1024,1024]{1,0:T(8,128)} collective-permute-done((f32[1024,1024]{1,0:T(8,128)}, f32[1024,1024]{1,0:T(8,128)}, u32[]{:S(2)}, u32[]{:S(2)}) %collective-permute-start.2) | collective-permute-done | bytes 4194336 | tf_op jit(solution)/shard_map/ppermute | solution.py:132
  738.9 89.9 %collective-permute-done = f32[1024,1024]{1,0:T(8,128)} collective-permute-done((f32[1024,1024]{1,0:T(8,128)}, f32[1024,1024]{1,0:T(8,128)}, u32[]{:S(2)}, u32[]{:S(2)}) %collective-permute-start) | collective-permute-done | bytes 4194336 | tf_op jit(solution)/shard_map/ppermute | solution.py:132
  828.8 12.4 %fusion.50 = (f32[1024]{0:T(1024)S(1)}, f32[1024]{0:T(1024)S(1)}, f32[1024]{0:T(1024)S(1)}, f32[1024]{0:T(1024)S(1)}, bf16[1,1024,1024]{2,1,0:T(8,128)(2,1)}) fusion(f32[1024,1024]{1,0:T(8,128)} %fusion.146, f32[1024]{0:T(1024)S(1)} %copy-done.166, bf16[2,1024,1024]{2,1,0:T(8,128)(2,1)} %param.18, f32[1024]{0:T(1024)S(1)} %copy-done.179, ...), kind=kLoop, calls=%fused_computation.80 | loop fusion | flops 19918848 | bytes 31485952 | tf_op jit(solution)/shard_map/reduce_sum | solution.py:244
  841.3 109.1 %psum.22 = f32[14688]{0:T(1024)S(1)} all-reduce(f32[14688]{0:T(1024)S(1)} %concatenate.226), channel_id=1, replica_groups=mesh['dp'=16,'tensor'=2] {'dp','tensor'}, use_global_device_ids=true, to_apply=%region_65.67 | all-reduce | flops 14688 | bytes 117504 | tf_op jit(solution)/shard_map/psum | solution.py:267
  953.6 12.2 %fusion.47 = (f32[1,1024,1024]{2,1,0:T(8,128)S(1)}, f32[1,1024,1024]{2,1,0:T(8,128)S(1)}, bf16[1,1024,1024]{2,1,0:T(8,128)(2,1)S(1)}) fusion(f32[1024]{0:T(1024)S(1)} %get-tuple-element.155, f32[1024]{0:T(1024)S(1)} %copy-done.212, f32[1024]{0:T(1024)S(1)} %copy-done.166, bf16[2,1024,1024]{2,1,0:T(8,128)(2,1)} %param.34, f32[1024]{0:T(1024)S(1)} %copy-done.179, ...), kind=kLoop, calls=%fused_computation.77 | loop fusion | flops 24117248 | bytes 44068864 | tf_op jit(solution)/shard_map/stack | solution.py:282
  978.9 16.4 %all-reduce.96.cloned.1.call-done = f32[64,256]{1,0:T(8,128)} async-done(((f32[64,256]{1,0:T(8,128)}), f32[64,256]{1,0:T(8,128)}) %all-reduce.96.cloned.1.call-update) | async-done | bytes 65552 | tf_op jit(solution)/shard_map/psum | solution.py:259
  (824 shorter events, 333.7 us)
Async XLA Ops:
  7.2 128.5 %copy-start = (bf16[1024,1024]{1,0:T(8,128)(2,1)S(1)}, bf16[1024,1024]{1,0:T(8,128)(2,1)}, u32[]{:S(2)}) copy-start(bf16[1024,1024]{1,0:T(8,128)(2,1)} %param.33) | copy-start | bytes 6291460
  7.2 965.3 %reduce-scatter.5.cloned.1.call-start = ((), (), s32[]{:S(2)}) async-start(), calls=%async_computation.2 | async-start | bytes 6127616 | tf_op jit(solution)/shard_map/reduce_scatter | solution.py:252
  16.0 19.6 %copy-start.50 = (bf16[1024,1024]{1,0:T(8,128)(2,1)}, bf16[1024,1024]{1,0:T(8,128)(2,1)S(1)}, u32[]{:S(2)}) copy-start(bf16[1024,1024]{1,0:T(8,128)(2,1)S(1)} %get-tuple-element.291) | copy-start | bytes 6291460
  27.2 223.9 %copy-start.4 = (f32[1024,256]{1,0:T(8,128)}, f32[1024,256]{1,0:T(8,128)S(1)}, u32[]{:S(2)}) copy-start(f32[1024,256]{1,0:T(8,128)S(1)} %fusion.472) | copy-start | bytes 3145732
  30.5 60.3 %copy-start.111 = (pred[128,128]{1,0:T(8,128)(4,1)}, pred[128,128]{1,0:T(8,128)(4,1)S(1)}, u32[]{:S(2)}) copy-start(pred[128,128]{1,0:T(8,128)(4,1)S(1)} %iota_compare_fusion.7) | copy-start | bytes 49156
  55.0 22.1 %copy-start.101 = (f32[2,8,8,128]{3,2,1,0:T(8,128)S(1)}, f32[2,8,8,128]{3,2,1,0:T(8,128)}, u32[]{:S(2)}) copy-start(f32[2,8,8,128]{3,2,1,0:T(8,128)} %get-tuple-element.333) | copy-start | bytes 196612
  55.0 22.1 %copy-start.216 = (f32[8,16]{1,0:T(8,128)S(1)}, f32[8,16]{1,0:T(8,128)}, u32[]{:S(2)}) copy-start(f32[8,16]{1,0:T(8,128)} %slice_reduce_fusion.2) | copy-start | bytes 1540
  175.2 22.8 %copy-start.6 = (f32[1024,256]{1,0:T(8,128)S(1)}, f32[1024,256]{1,0:T(8,128)}, u32[]{:S(2)}) copy-start(f32[1024,256]{1,0:T(8,128)} %fusion.479) | copy-start | bytes 3145732
  175.2 22.8 %copy-start.238 = (f32[256]{0:T(256)S(1)}, f32[256]{0:T(256)}, u32[]{:S(2)}) copy-start(f32[256]{0:T(256)} %param.28) | copy-start | bytes 3076
  211.6 27.3 %copy-start.173 = (f32[8,128]{1,0:T(8,128)}, f32[8,128]{1,0:T(8,128)S(1)}, u32[]{:S(2)}) copy-start(f32[8,128]{1,0:T(8,128)S(1)} %get-tuple-element.415) | copy-start | bytes 12292
  216.8 22.1 %copy-start.159 = (f32[8,16]{1,0:T(8,128)}, f32[8,16]{1,0:T(8,128)S(1)}, u32[]{:S(2)}) copy-start(f32[8,16]{1,0:T(8,128)S(1)} %slice_reduce_fusion) | copy-start | bytes 1540
  217.9 17.5 %copy-start.134 = (f32[1,1024]{1,0:T(1,128)}, f32[1,1024]{1,0:T(1,128)S(1)}, u32[]{:S(2)}) copy-start(f32[1,1024]{1,0:T(1,128)S(1)} %get-tuple-element.349) | copy-start | bytes 12292
  217.9 19.2 %copy-start.109 = (f32[1,1024]{1,0:T(1,128)}, f32[1,1024]{1,0:T(1,128)S(1)}, u32[]{:S(2)}) copy-start(f32[1,1024]{1,0:T(1,128)S(1)} %get-tuple-element.348) | copy-start | bytes 12292
  217.9 19.2 %copy-start.132 = (f32[1,1024]{1,0:T(1,128)}, f32[1,1024]{1,0:T(1,128)S(1)}, u32[]{:S(2)}) copy-start(f32[1,1024]{1,0:T(1,128)S(1)} %get-tuple-element.347) | copy-start | bytes 12292
  217.9 19.4 %copy-start.130 = (f32[1,1024]{1,0:T(1,128)}, f32[1,1024]{1,0:T(1,128)S(1)}, u32[]{:S(2)}) copy-start(f32[1,1024]{1,0:T(1,128)S(1)} %get-tuple-element.345) | copy-start | bytes 12292
  220.0 18.9 %copy-start.85 = (f32[8,128,16]{1,2,0:T(8,128)}, f32[8,128,16]{1,2,0:T(8,128)S(1)}, u32[]{:S(2)}) copy-start(f32[8,128,16]{1,2,0:T(8,128)S(1)} %copy.313) | copy-start | bytes 196612
  266.0 26.2 %copy-start.171 = (f32[8,128]{1,0:T(8,128)}, f32[8,128]{1,0:T(8,128)S(1)}, u32[]{:S(2)}) copy-start(f32[8,128]{1,0:T(8,128)S(1)} %get-tuple-element.426) | copy-start | bytes 12292
  271.7 20.5 %copy-start.157 = (f32[8,16]{1,0:T(8,128)}, f32[8,16]{1,0:T(8,128)S(1)}, u32[]{:S(2)}) copy-start(f32[8,16]{1,0:T(8,128)S(1)} %slice_reduce_fusion.1) | copy-start | bytes 1540
  272.5 18.1 %copy-start.123 = (f32[1,1024]{1,0:T(1,128)}, f32[1,1024]{1,0:T(1,128)S(1)}, u32[]{:S(2)}) copy-start(f32[1,1024]{1,0:T(1,128)S(1)} %get-tuple-element.354) | copy-start | bytes 12292
  272.5 18.3 %copy-start.121 = (f32[1,1024]{1,0:T(1,128)}, f32[1,1024]{1,0:T(1,128)S(1)}, u32[]{:S(2)}) copy-start(f32[1,1024]{1,0:T(1,128)S(1)} %get-tuple-element.352) | copy-start | bytes 12292
  273.5 18.7 %copy-start.83 = (f32[8,128,16]{1,2,0:T(8,128)}, f32[8,128,16]{1,2,0:T(8,128)S(1)}, u32[]{:S(2)}) copy-start(f32[8,128,16]{1,2,0:T(8,128)S(1)} %copy.294) | copy-start | bytes 196612
  517.0 460.0 %reduce-scatter.7.cloned.1.call-start = ((), (), s32[]{:S(2)}) async-start(), calls=%async_computation.4 | async-start | bytes 8912896
  544.0 451.4 %all-reduce.96.cloned.1.call-start = ((), (), s32[]{:S(2)}) async-start(), calls=%async_computation.3 | async-start | bytes 131072 | tf_op jit(solution)/shard_map/psum | solution.py:259
  555.2 93.8 %collective-permute-start.3 = (f32[1024,1024]{1,0:T(8,128)}, f32[1024,1024]{1,0:T(8,128)}, u32[]{:S(2)}, u32[]{:S(2)}) collective-permute-start(f32[1024,1024]{1,0:T(8,128)} %fusion.143), channel_id=1, source_target_pairs={{0,1},{1,0},{2,3},{3,2},{4,5},{5,4},{6,7},{7,6},{8,9},{9,8},{10,11... | collective-permute-start | bytes 12582920 | tf_op jit(solution)/shard_map/ppermute | solution.py:132
  563.2 175.7 %collective-permute-start.2 = (f32[1024,1024]{1,0:T(8,128)}, f32[1024,1024]{1,0:T(8,128)}, u32[]{:S(2)}, u32[]{:S(2)}) collective-permute-start(f32[1024,1024]{1,0:T(8,128)} %fusion.146), channel_id=1, source_target_pairs={{0,1},{1,0},{2,3},{3,2},{4,5},{5,4},{6,7},{7,6},{8,9},{9,8},{10,11... | collective-permute-start | bytes 12582920 | tf_op jit(solution)/shard_map/ppermute | solution.py:132
  569.9 258.9 %copy-start.164 = (f32[1024]{0:T(1024)S(1)}, f32[1024]{0:T(1024)}, u32[]{:S(2)}) copy-start(f32[1024]{0:T(1024)} %copy-done.163) | copy-start | bytes 12292
  569.9 258.9 %copy-start.166 = (f32[1024]{0:T(1024)S(1)}, f32[1024]{0:T(1024)}, u32[]{:S(2)}) copy-start(f32[1024]{0:T(1024)} %copy-done.165) | copy-start | bytes 12292
  569.9 258.9 %copy-start.179 = (f32[1024]{0:T(1024)S(1)}, f32[1024]{0:T(1024)}, u32[]{:S(2)}) copy-start(f32[1024]{0:T(1024)} %param.20) | copy-start | bytes 12292
  569.9 258.9 %collective-permute-start = (f32[1024,1024]{1,0:T(8,128)}, f32[1024,1024]{1,0:T(8,128)}, u32[]{:S(2)}, u32[]{:S(2)}) collective-permute-start(f32[1024,1024]{1,0:T(8,128)} %fusion.484), channel_id=1, source_target_pairs={{0,1},{1,0},{2,3},{3,2},{4,5},{5,4},{6,7},{7,6},{8,9},{9,8},{10,11... | collective-permute-start | bytes 12582920 | tf_op jit(solution)/shard_map/ppermute | solution.py:132
  574.5 379.1 %collective-permute-start.1 = (f32[1024,1024]{1,0:T(8,128)}, f32[1024,1024]{1,0:T(8,128)}, u32[]{:S(2)}, u32[]{:S(2)}) collective-permute-start(f32[1024,1024]{1,0:T(8,128)} %fusion.485), channel_id=1, source_target_pairs={{0,1},{1,0},{2,3},{3,2},{4,5},{5,4},{6,7},{7,6},{8,9},{9,8},{10,11... | collective-permute-start | bytes 12582920 | tf_op jit(solution)/shard_map/ppermute | solution.py:132
  577.4 376.2 %copy-start.211 = (f32[1024]{0:T(1024)S(1)}, f32[1024]{0:T(1024)}, u32[]{:S(2)}) copy-start(f32[1024]{0:T(1024)} %get-tuple-element.412) | copy-start | bytes 12292
  577.4 376.2 %copy-start.212 = (f32[1024]{0:T(1024)S(1)}, f32[1024]{0:T(1024)}, u32[]{:S(2)}) copy-start(f32[1024]{0:T(1024)} %get-tuple-element.457) | copy-start | bytes 12292
  (248 other events, 1442.9 us)
Sparse Core Ops, SparseCore 0:
  517.2 81.8 reduce-scatter.4
  603.1 103.8 reduce-scatter.6
  975.5 19.7 all-reduce.95
where the time goes:
time: 1020 us; the launch traced here: 1000 us
  waiting for transfers between devices  268 us (26%)
  matrix products  221 us (22%)
  other arithmetic  218 us (21%)
  local copies, waits for them, and re-layouts  156 us (15%)
  blocking collectives  119 us (12%)
  between operations  17.1 us (2%)
    ppermute x4, waiting for transfers between devices, tensor_sum(): return part + lax.ppermute(part, 'tensor', [(0, 1), (1, 0)])  251 us
    psum x1, blocking collectives, local(): lax.psum(jnp.concatenate([slots] + [g.reshape(-1) for g in shared]), ('dp...  109 us
    dot_general x6, matrix products, head_mix(): jnp.einsum('chts,cshp->cthp', mixing, low_head, preferred_element_type=jn...  50.1 us
    unnamed x564, local copies, waits for them, and re-layouts  46.9 us
    reduce_sum x8, other arithmetic, causal_conv(): weight[KERNEL - 1 - delay][None, :] * earlier * doc_masks[delay][:, None]  30 us
    convert_element_type x4, local copies, waits for them, and re-layouts, head_mix(): values.astype(jnp.bfloat16).reshape(chunks, CHUNK, heads, HEAD_DIM)  29.5 us
    reduce_sum x4, other arithmetic, head_mix(): return mixed + jnp.repeat(skip_gain, HEAD_DIM)[None, :] * values  27.6 us
    dot_general x6, matrix products, right_product(): lax.dot_general(left, weight, (((1,), (1,)), ((), ())), preferred_element...  27.1 us
  transfers between devices with their start and end apart: 7, of which 4 were waited for; matrix products, arithmetic and copies ran while one was open for 9% of the time, Pallas kernels for 0%

commit v1 on v0

--- a/solution.py
+++ b/solution.py
@@ -264,7 +264,12 @@
     place = lax.axis_index("tensor")
     mine = (jnp.arange(tensor_count) == place)[:, None]
     slots = jnp.where(mine, own_flat[None, :], 0.0).reshape(-1)
-    packed = lax.psum(jnp.concatenate([slots] + [g.reshape(-1) for g in shared]), ("dp", "tensor"))
+    packed = jnp.sum(
+        lax.all_gather(
+            jnp.concatenate([slots] + [g.reshape(-1) for g in shared]), ("dp", "tensor")
+        ),
+        axis=0,
+    )
     own_sum = lax.dynamic_slice(packed, (place * own_flat.shape[0],), (own_flat.shape[0],))
     shared_sum = packed[slots.shape[0] :]
 

time: 1020 us -> 977 us (0.958)
  blocking collectives: 119 us -> 9.69 us
  waiting for transfers between devices: 268 us -> 321 us
    psum x1 -> x0, blocking collectives: 109 us -> none  [local(): lax.psum(jnp.concatenate([slots] + [g.reshape(-1) for g in shared]), ('dp...]
    unnamed x4 -> x6, waiting for transfers between devices: 0.05 us -> 32.2 us
    ppermute x4, waiting for transfers between devices: 251 us -> 267 us  [tensor_sum(): return part + lax.ppermute(part, 'tensor', [(0, 1), (1, 0)])]
    unnamed x564 -> x520, local copies, waits for them, and re-layouts: 46.9 us -> 45.1 us
  transfers between devices with their start and end apart: 7 -> 8, of which waited for: 4 -> 6; matrix products, arithmetic and copies ran while one was open for 9% -> 25% of each run, Pallas kernels for 0% -> 0%
where the time goes in v1:
time: 977 us; the launch traced here: 965 us
  waiting for transfers between devices  321 us (33%)
  matrix products  225 us (23%)
  other arithmetic  221 us (23%)
  local copies, waits for them, and re-layouts  165 us (17%)
  between operations  19 us (2%)
    ppermute x4, waiting for transfers between devices, tensor_sum(): return part + lax.ppermute(part, 'tensor', [(0, 1), (1, 0)])  267 us
    dot_general x6, matrix products, head_mix(): jnp.einsum('chts,cshp->cthp', mixing, low_head, preferred_element_type=jn...  51.5 us
    unnamed x520, local copies, waits for them, and re-layouts  45.1 us
    unnamed x6, waiting for transfers between devices  32.2 us
    dot_general x6, matrix products, right_product(): lax.dot_general(left, weight, (((1,), (1,)), ((), ())), preferred_element...  30.8 us
    convert_element_type x4, local copies, waits for them, and re-layouts, head_mix(): values.astype(jnp.bfloat16).reshape(chunks, CHUNK, heads, HEAD_DIM)  29.5 us
    reduce_sum x8, other arithmetic, causal_conv(): weight[KERNEL - 1 - delay][None, :] * earlier * doc_masks[delay][:, None]  28.8 us
    reduce_sum x4, other arithmetic, head_mix(): return mixed + jnp.repeat(skip_gain, HEAD_DIM)[None, :] * values  27.3 us
  transfers between devices with their start and end apart: 8, of which 6 were waited for; matrix products, arithmetic and copies ran while one was open for 25% of the time, Pallas kernels for 0%

profile of v1, /device:TPU:0, one launch (start us, length us, event | category | flops | bytes accessed | tf_op | source)
XLA Modules:
  0.0 964.7 jit_solution(8225962138270703211)
XLA Ops:
  58.9 22.0 %fusion.446 = (bf16[1024,1024]{1,0:T(8,128)(2,1)}, f32[1024,1024]{1,0:T(8,128)}, bf16[1024,1024]{1,0:T(8,128)(2,1)}, f32[1024,1024]{1,0:T(8,128)S(1)}) fusion(f32[1024]{0:T(1024)S(1)} %get-tuple-element.459, f32[1021,1024]{1,0:T(8,128)} %bitcast.712, f32[1024]{0:T(1024)S(1)} %bitcast.949, f32[1024]{0:T(1024)S(1)} %get-tuple-element.458, ...), kind=kLoop, calls=%fused_computation.727 | loop fusion | flops 33554432 | bytes 46133248 | tf_op jit(solution)/shard_map/jvp()/convert_element_type | solution.py:64
  87.9 6.4 reshape.1880
  95.4 7.6 fusion.31
  118.4 6.5 reshape.1879
  125.0 7.6 fusion.30
  153.0 14.9 %multiply_reduce_fusion.15 = (f32[1024]{0:T(1024)S(1)}, f32[1024]{0:T(1024)S(1)}, f32[1024,1024]{1,0:T(8,128)}, f32[1024]{0:T(1024)S(1)}, f32[1024]{0:T(1024)S(1...) fusion(f32[1024]{0:T(1024)S(1)} %copy-done.218, f32[1024,1024]{1,0:T(8,128)} %fusion.476, ...), kind=kOutput, calls=%fused_computation.180 | convolution fusion | flops 2172645376 | bytes 46161920 | tf_op jit(solution)/shard_map/dot_general | solution.py:194
  167.9 9.7 %psum.14 = f32[4,1024]{1,0:T(4,128)S(1)} all-reduce(f32[4,1024]{1,0:T(4,128)S(1)} %pad_maximum_fusion.9), channel_id=1, replica_groups=mesh['dp'=16,'tensor'=2] {'tensor'}, use_global_device_ids=true, to_apply=%region_6.7 | all-reduce | flops 4096 | bytes 32768 | tf_op jit(solution)/shard_map/psum | solution.py:197
  177.7 21.0 %multiply_multiply_fusion.1 = (f32[1024,1024]{1,0:T(8,128)}, bf16[1024,1024]{1,0:T(8,128)(2,1)}, f32[1024]{0:T(1024)}, bf16[1024,1024]{1,0:T(8,128)(2,1)}, bf16[...) fusion(f32[1024,1024]{1,0:T(8,128)} %fusion.476, ...), kind=kLoop, calls=%fused_computation.163 | loop fusion | flops 54523904 | bytes 58761216 | tf_op jit(solution)/shard_map/mul | solution.py:212
  222.4 13.6 %multiply_reduce_fusion.2 = (f32[1024]{0:T(1024)}, f32[1024,1024]{1,0:T(8,128)S(1)}, f32[1024,1024]{1,0:T(8,128)}) fusion(f32[1024,1024]{1,0:T(8,128)} %get-tuple-element.60, f32[1024]{0:T(1024)} %copy-done.134, f32[1021,1024]{1,0:T(8,128)} %bitcast.724, f32[1024]{0:T(1024)} %bitcast.924, f32[1024]{0:T(1024)} %copy-done.125, f32[1022,1024]{1,0:T(8,128)} %bitcast.725, ...), kind=kLoop, calls=%fused_computation.124 | loop fusion | flops 17824768 | bytes 29372416 | tf_op jit(solution)/shard_map/transpose(jvp(jvp()))/checkpoint/reduce_sum | solution.py:93
  264.3 7.1 copy.348
  271.4 7.6 reshape.1883
  281.7 9.4 multiply_reduce_fusion.7
  304.8 6.3 reshape.1884
  311.2 12.1 %fusion.17 = (f32[8,16,128]{2,1,0:T(8,128)}, f32[8,16,128]{2,1,0:T(8,128)}, f32[8,16,128]{2,1,0:T(8,128)S(1)}, bf16[8,128,128]{2,1,0:T(8,128)(2,1)S(1)}) fusion(f32[8,16,128]{2,1,0:T(8,128)} %copy.315, f32[8,128,128]{2,1,0:T(8,128)} %fusion.491, f32[8,16,128]{2,1,0:T(8,128)S(1)} %fusion.299, pred[8,128,128]{2,1,0:T(8,128)(4,1)} %copy-done.105, ...), kind=kOutput, calls=%fused_computation.41 | convolution fusion | flops 297615360 | bytes 5439488 | tf_op jit(solution)/shard_map/transpose(jvp(jvp()))/checkpoint/chts,cshp->cthp/dot_general | solution.py:65
  352.0 6.3 fusion.432
  390.3 13.5 %multiply_reduce_fusion.3 = (f32[1024]{0:T(1024)}, f32[1024,1024]{1,0:T(8,128)S(1)}, f32[1024,1024]{1,0:T(8,128)}) fusion(f32[1024,1024]{1,0:T(8,128)} %get-tuple-element.46, f32[1024]{0:T(1024)} %copy-done.137, f32[1021,1024]{1,0:T(8,128)} %bitcast.715, f32[1024]{0:T(1024)} %bitcast.926, f32[1024]{0:T(1024)} %copy-done.131, f32[1022,1024]{1,0:T(8,128)} %bitcast.716, ...), kind=kLoop, calls=%fused_computation.125 | loop fusion | flops 17824768 | bytes 29372416 | tf_op jit(solution)/shard_map/transpose(jvp(jvp()))/checkpoint/reduce_sum | solution.py:93
  428.3 7.1 copy.345
  435.4 7.6 reshape.1881
  445.7 9.3 multiply_reduce_fusion.11
  468.9 6.3 reshape.1882
  475.3 12.3 %fusion.15 = (f32[8,16,128]{2,1,0:T(8,128)}, f32[8,16,128]{2,1,0:T(8,128)}, f32[8,16,128]{2,1,0:T(8,128)S(1)}, bf16[8,128,128]{2,1,0:T(8,128)(2,1)S(1)}) fusion(f32[8,16,128]{2,1,0:T(8,128)} %copy.296, f32[8,128,128]{2,1,0:T(8,128)} %fusion.487, f32[8,16,128]{2,1,0:T(8,128)S(1)} %fusion.302, pred[8,128,128]{2,1,0:T(8,128)(4,1)} %get-tuple-element.374, ...), kind=kOutput, calls=%fused_computation.39 | convolution fusion | flops 297615360 | bytes 5439488 | tf_op jit(solution)/shard_map/transpose(jvp(jvp()))/checkpoint/chts,cshp->cthp/dot_general | solution.py:65
  537.2 86.1 %collective-permute-done.2 = f32[1024,1024]{1,0:T(8,128)} collective-permute-done((f32[1024,1024]{1,0:T(8,128)}, f32[1024,1024]{1,0:T(8,128)}, u32[]{:S(2)}, u32[]{:S(2)}) %collective-permute-start.2) | collective-permute-done | bytes 4194336 | tf_op jit(solution)/shard_map/ppermute | solution.py:132
  623.3 87.0 %collective-permute-done = f32[1024,1024]{1,0:T(8,128)} collective-permute-done((f32[1024,1024]{1,0:T(8,128)}, f32[1024,1024]{1,0:T(8,128)}, u32[]{:S(2)}, u32[]{:S(2)}) %collective-permute-start) | collective-permute-done | bytes 4194336 | tf_op jit(solution)/shard_map/ppermute | solution.py:132
  710.3 12.4 %fusion.50 = (f32[1024]{0:T(1024)S(1)}, f32[1024]{0:T(1024)S(1)}, f32[1024]{0:T(1024)S(1)}, f32[1024]{0:T(1024)S(1)}, bf16[1,1024,1024]{2,1,0:T(8,128)(2,1)}) fusion(f32[1024,1024]{1,0:T(8,128)} %fusion.146, f32[1024]{0:T(1024)S(1)} %copy-done.148, bf16[2,1024,1024]{2,1,0:T(8,128)(2,1)} %param.18, f32[1024]{0:T(1024)S(1)} %copy-done.157, ...), kind=kLoop, calls=%fused_computation.80 | loop fusion | flops 19918848 | bytes 31485952 | tf_op jit(solution)/shard_map/reduce_sum | solution.py:244
  725.9 12.7 %fusion.18 = f32[1024,1296]{1,0:T(8,128)} fusion(bf16[1024,16]{1,0:T(8,128)(2,1)S(1)} %copy-done.91, bf16[1024,256]{1,0:T(8,128)(2,1)S(1)} %copy-done.80, bf16[1024,1024]{1,0:T(8,128)(2,1)} %copy-done.70, bf16[1024,16]{1,0:T(8,128)(2,1)} %copy-done.92, bf16[1024,256]{1,0:T(8,128)(2,1)S(1)} %copy-done.82, bf16[1024,1024]{1,0:T(8,128)(2,1)} %copy-done.71, ...), kind=kOutput, calls=%fused_computation.44 | convolution fusion | flops 5476057088 | bytes 14811136 | tf_op jit(solution)/shard_map/dot_general | solution.py:122
  739.0 8.2 fusion.62
  756.2 9.4 copy.351
  773.3 94.2 %collective-permute-done.1 = f32[1024,1024]{1,0:T(8,128)} collective-permute-done((f32[1024,1024]{1,0:T(8,128)}, f32[1024,1024]{1,0:T(8,128)}, u32[]{:S(2)}, u32[]{:S(2)}) %collective-permute-start.1) | collective-permute-done | bytes 4194336 | tf_op jit(solution)/shard_map/ppermute | solution.py:132
  867.5 12.6 %fusion.47 = (f32[1,1024,1024]{2,1,0:T(8,128)S(1)}, f32[1,1024,1024]{2,1,0:T(8,128)S(1)}, bf16[1,1024,1024]{2,1,0:T(8,128)(2,1)S(1)}) fusion(f32[1024]{0:T(1024)S(1)} %get-tuple-element.155, f32[1024]{0:T(1024)S(1)} %copy-done.184, f32[1024]{0:T(1024)S(1)} %copy-done.148, bf16[2,1024,1024]{2,1,0:T(8,128)(2,1)} %param.34, f32[1024]{0:T(1024)S(1)} %copy-done.157, ...), kind=kLoop, calls=%fused_computation.77 | loop fusion | flops 24117248 | bytes 44068864 | tf_op jit(solution)/shard_map/stack | solution.py:287
  886.7 18.9 %all-reduce.100.cloned.1.call-done = f32[470016]{0:T(1024)} async-done(((f32[470016]{0:T(1024)}), f32[470016]{0:T(1024)}) %all-reduce.100.cloned.1.call-update) | async-done | bytes 1880080
  919.0 13.2 %reduce-scatter.7.cloned.1.call-done = f32[64,2048]{1,0:T(8,128)} async-done(((f32[1024,2048]{1,0:T(8,128)}), f32[64,2048]{1,0:T(8,128)}) %reduce-scatter.7.cloned.1.call-update) | async-done | bytes 524304
  934.1 21.1 %all-reduce.98.cloned.1.call-done = f32[64,256]{1,0:T(8,128)} async-done(((f32[64,256]{1,0:T(8,128)}), f32[64,256]{1,0:T(8,128)}) %all-reduce.98.cloned.1.call-update) | async-done | bytes 65552 | tf_op jit(solution)/shard_map/psum | solution.py:259
  (784 shorter events, 355.5 us)
Async XLA Ops:
  8.0 130.1 %copy-start = (bf16[1024,1024]{1,0:T(8,128)(2,1)S(1)}, bf16[1024,1024]{1,0:T(8,128)(2,1)}, u32[]{:S(2)}) copy-start(bf16[1024,1024]{1,0:T(8,128)(2,1)} %param.33) | copy-start | bytes 6291460
  8.0 897.6 %all-reduce.100.cloned.1.call-start = ((), (), s32[]{:S(2)}) async-start(), calls=%async_computation.4 | async-start | bytes 3760128
  18.6 17.5 %copy-start.47 = (bf16[1024,1024]{1,0:T(8,128)(2,1)}, bf16[1024,1024]{1,0:T(8,128)(2,1)S(1)}, u32[]{:S(2)}) copy-start(bf16[1024,1024]{1,0:T(8,128)(2,1)S(1)} %get-tuple-element.290) | copy-start | bytes 6291460
  18.6 21.9 %copy-start.48 = (bf16[1024,1024]{1,0:T(8,128)(2,1)}, bf16[1024,1024]{1,0:T(8,128)(2,1)S(1)}, u32[]{:S(2)}) copy-start(bf16[1024,1024]{1,0:T(8,128)(2,1)S(1)} %get-tuple-element.291) | copy-start | bytes 6291460
  28.3 17.2 %copy-start.77 = (f32[1024,16]{0,1:T(8,128)}, f32[1024,16]{0,1:T(8,128)S(1)}, u32[]{:S(2)}) copy-start(f32[1024,16]{0,1:T(8,128)S(1)} %fusion.471) | copy-start | bytes 196612
  31.0 18.8 %copy-start.5 = (f32[1024,256]{1,0:T(8,128)}, f32[1024,256]{1,0:T(8,128)S(1)}, u32[]{:S(2)}) copy-start(f32[1024,256]{1,0:T(8,128)S(1)} %fusion.472) | copy-start | bytes 3145732
  58.9 22.1 %copy-start.189 = (f32[8,16]{1,0:T(8,128)S(1)}, f32[8,16]{1,0:T(8,128)}, u32[]{:S(2)}) copy-start(f32[8,16]{1,0:T(8,128)} %copy-done.188) | copy-start | bytes 1540
  177.6 22.3 %copy-start.7 = (f32[1024,256]{1,0:T(8,128)S(1)}, f32[1024,256]{1,0:T(8,128)}, u32[]{:S(2)}) copy-start(f32[1024,256]{1,0:T(8,128)} %fusion.479) | copy-start | bytes 3145732
  177.6 22.3 %copy-start.210 = (f32[256]{0:T(256)S(1)}, f32[256]{0:T(256)}, u32[]{:S(2)}) copy-start(f32[256]{0:T(256)} %param.28) | copy-start | bytes 3076
  311.2 12.4 %copy-start.107 = (f32[1,1024]{1,0:T(1,128)S(1)}, f32[1,1024]{1,0:T(1,128)}, u32[]{:S(2)}) copy-start(f32[1,1024]{1,0:T(1,128)} %get-tuple-element.343) | copy-start | bytes 12292
  366.6 170.6 %collective-permute-start.3 = (f32[1024,1024]{1,0:T(8,128)}, f32[1024,1024]{1,0:T(8,128)}, u32[]{:S(2)}, u32[]{:S(2)}) collective-permute-start(f32[1024,1024]{1,0:T(8,128)} %fusion.143), channel_id=1, source_target_pairs={{0,1},{1,0},{2,3},{3,2},{4,5},{5,4},{6,7},{7,6},{8,9},{9,8},{10,11... | collective-permute-start | bytes 12582920 | tf_op jit(solution)/shard_map/ppermute | solution.py:132
  475.3 12.6 %copy-start.14 = (f32[8,128,1024]{2,1,0:T(8,128)S(1)}, f32[8,128,1024]{2,1,0:T(8,128)}, u32[]{:S(2)}) copy-start(f32[8,128,1024]{2,1,0:T(8,128)} %fusion.488) | copy-start | bytes 12582916
  475.3 12.6 %copy-start.26 = (bf16[8,128,1024]{2,1,0:T(8,128)(2,1)S(1)}, bf16[8,128,1024]{2,1,0:T(8,128)(2,1)}, u32[]{:S(2)}) copy-start(bf16[8,128,1024]{2,1,0:T(8,128)(2,1)} %copy-done.24) | copy-start | bytes 6291460
  475.3 12.6 %copy-start.115 = (f32[1,1024]{1,0:T(1,128)S(1)}, f32[1,1024]{1,0:T(1,128)}, u32[]{:S(2)}) copy-start(f32[1,1024]{1,0:T(1,128)} %get-tuple-element.351) | copy-start | bytes 12292
  475.3 12.6 %copy-start.117 = (f32[1,1024]{1,0:T(1,128)S(1)}, f32[1,1024]{1,0:T(1,128)}, u32[]{:S(2)}) copy-start(f32[1,1024]{1,0:T(1,128)} %get-tuple-element.352) | copy-start | bytes 12292
  475.3 12.6 %copy-start.119 = (f32[1,1024]{1,0:T(1,128)S(1)}, f32[1,1024]{1,0:T(1,128)}, u32[]{:S(2)}) copy-start(f32[1,1024]{1,0:T(1,128)} %get-tuple-element.354) | copy-start | bytes 12292
  475.3 12.6 %copy-start.121 = (f32[1,1024]{1,0:T(1,128)S(1)}, f32[1,1024]{1,0:T(1,128)}, u32[]{:S(2)}) copy-start(f32[1,1024]{1,0:T(1,128)} %get-tuple-element.356) | copy-start | bytes 12292
  529.4 93.8 %collective-permute-start.2 = (f32[1024,1024]{1,0:T(8,128)}, f32[1024,1024]{1,0:T(8,128)}, u32[]{:S(2)}, u32[]{:S(2)}) collective-permute-start(f32[1024,1024]{1,0:T(8,128)} %fusion.146), channel_id=1, source_target_pairs={{0,1},{1,0},{2,3},{3,2},{4,5},{5,4},{6,7},{7,6},{8,9},{9,8},{10,11... | collective-permute-start | bytes 12582920 | tf_op jit(solution)/shard_map/ppermute | solution.py:132
  531.7 178.6 %copy-start.146 = (f32[1024]{0:T(1024)S(1)}, f32[1024]{0:T(1024)}, u32[]{:S(2)}) copy-start(f32[1024]{0:T(1024)} %copy-done.145) | copy-start | bytes 12292
  531.7 178.6 %copy-start.148 = (f32[1024]{0:T(1024)S(1)}, f32[1024]{0:T(1024)}, u32[]{:S(2)}) copy-start(f32[1024]{0:T(1024)} %copy-done.147) | copy-start | bytes 12292
  531.7 178.6 %copy-start.157 = (f32[1024]{0:T(1024)S(1)}, f32[1024]{0:T(1024)}, u32[]{:S(2)}) copy-start(f32[1024]{0:T(1024)} %param.20) | copy-start | bytes 12292
  536.1 174.2 %collective-permute-start = (f32[1024,1024]{1,0:T(8,128)}, f32[1024,1024]{1,0:T(8,128)}, u32[]{:S(2)}, u32[]{:S(2)}) collective-permute-start(f32[1024,1024]{1,0:T(8,128)} %fusion.484), channel_id=1, source_target_pairs={{0,1},{1,0},{2,3},{3,2},{4,5},{5,4},{6,7},{7,6},{8,9},{9,8},{10,11... | collective-permute-start | bytes 12582920 | tf_op jit(solution)/shard_map/ppermute | solution.py:132
  537.1 188.8 %copy-start.80 = (bf16[1024,256]{1,0:T(8,128)(2,1)S(1)}, bf16[1024,256]{1,0:T(8,128)(2,1)}, u32[]{:S(2)}) copy-start(bf16[1024,256]{1,0:T(8,128)(2,1)} %copy-done.79) | copy-start | bytes 1572868
  537.1 188.8 %copy-start.82 = (bf16[1024,256]{1,0:T(8,128)(2,1)S(1)}, bf16[1024,256]{1,0:T(8,128)(2,1)}, u32[]{:S(2)}) copy-start(bf16[1024,256]{1,0:T(8,128)(2,1)} %copy-done.81) | copy-start | bytes 1572868
  537.1 188.8 %copy-start.91 = (bf16[1024,16]{1,0:T(8,128)(2,1)S(1)}, bf16[1024,16]{1,0:T(8,128)(2,1)}, u32[]{:S(2)}) copy-start(bf16[1024,16]{1,0:T(8,128)(2,1)} %copy-done.90) | copy-start | bytes 98308
  725.8 188.6 %reduce-scatter.5.cloned.1.call-start = ((), (), s32[]{:S(2)}) async-start(), calls=%async_computation.2 | async-start | bytes 6127616 | tf_op jit(solution)/shard_map/reduce_scatter | solution.py:252
  738.7 193.5 %reduce-scatter.7.cloned.1.call-start = ((), (), s32[]{:S(2)}) async-start(), calls=%async_computation.5 | async-start | bytes 8912896
  765.7 101.9 %copy-start.183 = (f32[1024]{0:T(1024)S(1)}, f32[1024]{0:T(1024)}, u32[]{:S(2)}) copy-start(f32[1024]{0:T(1024)} %get-tuple-element.412) | copy-start | bytes 12292
  765.7 101.9 %copy-start.184 = (f32[1024]{0:T(1024)S(1)}, f32[1024]{0:T(1024)}, u32[]{:S(2)}) copy-start(f32[1024]{0:T(1024)} %get-tuple-element.457) | copy-start | bytes 12292
  765.7 189.5 %all-reduce.98.cloned.1.call-start = ((), (), s32[]{:S(2)}) async-start(), calls=%async_computation.3 | async-start | bytes 131072 | tf_op jit(solution)/shard_map/psum | solution.py:259
  772.0 95.5 %collective-permute-start.1 = (f32[1024,1024]{1,0:T(8,128)}, f32[1024,1024]{1,0:T(8,128)}, u32[]{:S(2)}, u32[]{:S(2)}) collective-permute-start(f32[1024,1024]{1,0:T(8,128)} %fusion.485), channel_id=1, source_target_pairs={{0,1},{1,0},{2,3},{3,2},{4,5},{5,4},{6,7},{7,6},{8,9},{9,8},{10,11... | collective-permute-start | bytes 12582920 | tf_op jit(solution)/shard_map/ppermute | solution.py:132
  867.5 12.6 %copy-start.49 = (bf16[1,1024,1024]{2,1,0:T(8,128)(2,1)S(1)}, bf16[1,1024,1024]{2,1,0:T(8,128)(2,1)}, u32[]{:S(2)}) copy-start(bf16[1,1024,1024]{2,1,0:T(8,128)(2,1)} %get-tuple-element.295) | copy-start | bytes 6291460
  (226 other events, 1105.1 us)
Sparse Core Ops, SparseCore 0:
  726.0 179.6 all-reduce.99
Sparse Core Ops, SparseCore 1:
  738.8 83.3 reduce-scatter.4
  826.1 106.1 reduce-scatter.6
  934.9 20.2 all-reduce.97
